TPU v7x, 512 devices: a whole 4x4x16 slice. The times are simulated.
512 devices in a mesh: expert: 32 (over x_lo, z), tensor: 16 (over y, x_hi, core).
Axes of the slice: x: 4 (x_hi: 2, x_lo: 2; x = x_hi * 2 + x_lo), y: 4, z: 16, core: 2. Of those that a mesh axis runs over, the one named last changes fastest.
Arguments:
- tokens: bfloat16 [1536, 5120], P('expert', 'tensor'), may hold values from -6 to 6
- expert_ids: int32 [1536, 6], P('expert'), may hold values from 0 to 31, all different within a row; in each aligned block of 48 rows (0 to 47, 48 to 95, ...) at most 18 rows name the same one
- route_weights: float32 [1536, 6], P('expert'), may hold values from 0.05 to 0.6
- routed_gate: bfloat16 [32, 1536, 5120], P('expert', 'tensor'), may hold values from -0.078125 to 0.078125
- routed_up: bfloat16 [32, 1536, 5120], P('expert', 'tensor'), may hold values from -0.078125 to 0.078125
- routed_down: bfloat16 [32, 1536, 5120], P('expert', None, 'tensor'), may hold values from -0.15625 to 0.15625
- shared_gate: bfloat16 [5120, 3072], P('expert', 'tensor'), may hold values from -0.078125 to 0.078125
- shared_up: bfloat16 [5120, 3072], P('expert', 'tensor'), may hold values from -0.078125 to 0.078125
- shared_down: bfloat16 [3072, 5120], P('tensor', 'expert'), may hold values from -0.21875 to 0.21875
- norm_gain: float32 [5120], replicated, may hold values from 0.25 to 1.75
- proj_weight: bfloat16 [2112, 5120], P('tensor'), may hold values from -0.078125 to 0.078125
Outputs:
- stream: bfloat16 [1536, 5120], P('expert', 'tensor')
- projected: bfloat16 [1536, 2112], P('expert', 'tensor')
Inputs may be any that keep to these rules, and one draw needn't show every extreme that they name: `expert_ids`: in each aligned block of 48 tokens (those of one index of expert) no expert is chosen by more than 18 tokens, and some expert is chosen by exactly 18; a token's 6 experts differ.
All inputs are finite; a program needn't handle non-finite values.
Results may differ from a plain program's by a relative error of at most 0.019.
Values may be sent and summed in bfloat16 or wider, within the bound.
No kernel may reach another device: no remote copies, remote signals or barrier semaphores. Data moves between devices by JAX's collectives and lax.ppermute only.
A program may use at most 128 MiB of HBM per device.

v0:
```python
import jax
import jax.numpy as jnp
from jax import lax
from jax.sharding import PartitionSpec as P


def swiglu(gate, up):
    return (jax.nn.silu(gate) * up).astype(jnp.bfloat16)


def dot_rows(left, right):
    return lax.dot_general(
        left, right, (((1,), (1,)), ((), ())), preferred_element_type=jnp.float32
    )


def per_device(
    tokens,
    expert_ids,
    route_weights,
    routed_gate,
    routed_up,
    routed_down,
    shared_gate,
    shared_up,
    shared_down,
    norm_gain,
    proj_weight,
):
    tok_rows = tokens.shape[0]
    local_width = tokens.shape[1]
    top = expert_ids.shape[1]
    experts = lax.axis_size("expert")
    capacity = min(tok_rows, 2 * tok_rows * top // experts)
    features = lax.all_gather(tokens, "tensor", axis=1, tiled=True)
    flat_ids = expert_ids.reshape(-1)
    onehot = (flat_ids[:, None] == jnp.arange(experts, dtype=jnp.int32)[None, :]).astype(jnp.int32)
    slots = jnp.sum((jnp.cumsum(onehot, axis=0) - onehot) * onehot, axis=1)
    target = flat_ids * capacity + slots
    owners = jnp.repeat(jnp.arange(tok_rows, dtype=jnp.int32), top)
    sources = jnp.full((experts * capacity,), tok_rows, jnp.int32).at[target].set(owners)
    gate_w = routed_gate[0]
    up_w = routed_up[0]
    down_w = routed_down[0]
    padded = jnp.concatenate([features, jnp.zeros((1, features.shape[1]), features.dtype)], axis=0)
    outgoing = padded[sources].reshape(experts, capacity, features.shape[1])
    arrived = lax.all_to_all(outgoing, "expert", split_axis=0, concat_axis=0, tiled=True)
    count = arrived.shape[1]
    rows = arrived.reshape(-1, arrived.shape[2])
    hidden = swiglu(dot_rows(rows, gate_w), dot_rows(rows, up_w))
    hidden_all = lax.all_gather(hidden, "tensor", axis=1, tiled=True)
    result = jnp.dot(hidden_all, down_w, preferred_element_type=jnp.float32).astype(jnp.bfloat16)
    result = result.reshape(experts, count, result.shape[1])
    returned = lax.all_to_all(result, "expert", split_axis=0, concat_axis=0, tiled=True)
    flat_back = returned.reshape(experts * capacity, returned.shape[2])
    picked = flat_back[target].reshape(tok_rows, top, returned.shape[2]).astype(jnp.float32)
    routed = jnp.sum(picked * route_weights[:, :, None], axis=1)
    gate_sum = jnp.dot(
        features,
        lax.all_gather(shared_gate, "expert", axis=0, tiled=True),
        preferred_element_type=jnp.float32,
    )
    up_sum = jnp.dot(
        features,
        lax.all_gather(shared_up, "expert", axis=0, tiled=True),
        preferred_element_type=jnp.float32,
    )
    shared_hidden = swiglu(gate_sum, up_sum)
    shared_terms = jnp.dot(
        shared_hidden,
        lax.all_gather(shared_down, "expert", axis=1, tiled=True),
        preferred_element_type=jnp.float32,
    )
    rank = lax.axis_index("tensor")
    shared_full = lax.psum(shared_terms.astype(jnp.bfloat16), "tensor").astype(jnp.float32)
    shared_mine = lax.dynamic_slice_in_dim(shared_full, rank * local_width, local_width, 1)
    stream = (tokens.astype(jnp.float32) + shared_mine + routed).astype(jnp.bfloat16)
    stream_all = lax.all_gather(stream, "tensor", axis=1, tiled=True)
    values = stream_all.astype(jnp.float32)
    scale = lax.rsqrt(jnp.mean(values * values, axis=1, keepdims=True) + 1e-06)
    normed = (values * scale * norm_gain[None, :]).astype(jnp.bfloat16)
    projected = dot_rows(normed, proj_weight).astype(jnp.bfloat16)
    return (stream, projected)


def solution(mesh):
    in_specs = (
        P("expert", "tensor"),
        P("expert", None),
        P("expert", None),
        P("expert", "tensor", None),
        P("expert", "tensor", None),
        P("expert", None, "tensor"),
        P("expert", "tensor"),
        P("expert", "tensor"),
        P("tensor", "expert"),
        P(),
        P("tensor", None),
    )
    out_specs = (P("expert", "tensor"), P("expert", "tensor"))
    return jax.shard_map(
        per_device, mesh=mesh, in_specs=in_specs, out_specs=out_specs, check_vma=False
    )
```

profile of v0, /device:TPU:1, one launch (start us, length us, event | category | flops | bytes accessed | tf_op | source)
XLA Modules:
  0.0 1078.2 jit_solution(14754052590517255412)
XLA Ops:
  7.2 0.9 copy.26
  8.1 0.7 broadcast_multiply_fusion
  8.9 0.9 reduce-window.6
  10.6 2.9 scatter_custom_fusion
  13.5 29.4 %all-gather = bf16[16,320,48]{1,2,0:T(8,128)(2,1)S(1)} all-gather(bf16[1,320,48]{1,2,0:T(8,128)(2,1)} %bitcast.43), channel_id=1, replica_groups=mesh['expert'=32,'tensor'=16] {'tensor'}, dimensions={0}, use_global_device_ids=true | all-gather | bytes 522240 | tf_op jit(solution)/shard_map/all_gather | solution.py:35
  43.1 0.4 reshape.108
  43.6 6.0 gather_fusion
  49.6 8.5 reshape.76
  58.1 359.3 %all_to_all.10 = bf16[32,18,5120]{2,1,0:T(8,128)(2,1)} all-to-all(bf16[32,18,5120]{2,1,0:T(8,128)(2,1)} %reshape.76), channel_id=1, replica_groups=mesh['expert'=32,'tensor'=16] {'expert'}, dimensions={0} | all-to-all | bytes 11796480 | tf_op jit(solution)/shard_map/all_to_all | solution.py:47
  417.4 8.8 reshape.77
  426.2 4.8 fusion.4
  431.1 2.6 fusion
  433.8 0.7 all-gather.7.cloned.1.call-update
  434.5 0.7 all-gather.11.cloned.1.call-update
  435.3 0.5 all-gather.9.cloned.1.call-update
  435.8 51.4 %all-gather.13.cloned.1.call-done = bf16[576,1536]{0,1:T(8,128)(2,1)} async-done(((bf16[576,96]{0,1:T(8,128)(2,1)}), bf16[576,1536]{0,1:T(8,128)(2,1)}) %all-gather.13.cloned.1.call-update) | async-done | bytes 1769488 | tf_op jit(solution)/shard_map/all_gather | solution.py:51
  487.2 2.8 convolution_convert_fusion.1
  490.0 0.2 copy.29
  490.2 1.0 reshape.78
  491.3 12.3 %all-to-all-start.1 = ((bf16[32,18,320]{2,1,0:T(8,128)(2,1)}), bf16[32,18,320]{2,1,0:T(8,128)(2,1)S(1)}, u32[]{:S(2)}, u32[]{:S(2)}) async-start(bf16[32,18,320]{2,1,0:T(8,128)(2,1)} %reshape.78), calls=%async_computation.1 | async-start | bytes 1179648 | tf_op jit(solution)/shard_map/all_to_all | solution.py:54
  503.8 110.9 %all-gather.7.cloned.1.call-done = bf16[5120,192]{1,0:T(8,128)(2,1)} async-done(((bf16[160,192]{1,0:T(8,128)(2,1)}), bf16[5120,192]{1,0:T(8,128)(2,1)}) %all-gather.7.cloned.1.call-update) | async-done | bytes 1966096 | tf_op jit(solution)/shard_map/all_gather | solution.py:60
  614.7 2.3 fusion.20
  617.0 123.6 %all-gather.11.cloned.1.call-done = bf16[192,5120]{0,1:T(8,128)(2,1)} async-done(((bf16[192,160]{0,1:T(8,128)(2,1)}), bf16[192,5120]{0,1:T(8,128)(2,1)}) %all-gather.11.cloned.1.call-update) | async-done | bytes 1966096 | tf_op jit(solution)/shard_map/all_gather | solution.py:71
  740.7 130.1 %all-gather.9.cloned.1.call-done = bf16[5120,192]{1,0:T(8,128)(2,1)} async-done(((bf16[160,192]{1,0:T(8,128)(2,1)}), bf16[5120,192]{1,0:T(8,128)(2,1)}) %all-gather.9.cloned.1.call-update) | async-done | bytes 1966096 | tf_op jit(solution)/shard_map/all_gather | solution.py:65
  870.8 5.2 convolution_convert_fusion
  876.4 2.0 gather_fusion.1
  878.4 0.2 multiply_reduce_fusion.1
  878.7 161.6 %all-reduce.4.cloned.1.call-done = bf16[48,5120]{1,0:T(8,128)(2,1)} async-done(((bf16[48,5120]{1,0:T(8,128)(2,1)}), bf16[48,5120]{1,0:T(8,128)(2,1)}) %all-reduce.4.cloned.1.call-update) | async-done | bytes 491536 | tf_op jit(solution)/shard_map/psum | solution.py:75
  1040.3 0.9 add_convert_fusion
  1041.2 27.8 %all-gather.1 = bf16[16,320,48]{1,2,0:T(8,128)(2,1)S(1)} all-gather(bf16[1,320,48]{1,2,0:T(8,128)(2,1)S(1)} %bitcast.44), channel_id=1, replica_groups=mesh['expert'=32,'tensor'=16] {'tensor'}, dimensions={0}, use_global_device_ids=true | all-gather | bytes 522240 | tf_op jit(solution)/shard_map/all_gather | solution.py:78
  1069.1 0.3 reshape.111
  1069.7 2.0 convolution_convert_fusion.2
  (45 shorter events, 2.2 us)
Async XLA Ops:
  7.2 1062.5 %copy-start = (bf16[132,5120]{1,0:T(8,128)(2,1)S(1)}, bf16[132,5120]{1,0:T(8,128)(2,1)}, u32[]{:S(2)}) copy-start(bf16[132,5120]{1,0:T(8,128)(2,1)} %param.21) | copy-start | bytes 4055044
  7.2 480.0 %all-gather.13.cloned.1.call-start = ((), (), s32[]{:S(2)}) async-start(), calls=%async_computation.6 | async-start | bytes 2088960 | tf_op jit(solution)/shard_map/all_gather | solution.py:51
  417.4 8.8 copy-start.2
  426.2 4.8 copy-start.1
  426.2 4.8 copy-start.6
  433.7 181.0 %all-gather.7.cloned.1.call-start = ((), (), s32[]{:S(2)}) async-start(), calls=%async_computation.2 | async-start | bytes 2703360 | tf_op jit(solution)/shard_map/all_gather | solution.py:60
  434.5 306.2 %all-gather.11.cloned.1.call-start = ((), (), s32[]{:S(2)}) async-start(), calls=%async_computation.4 | async-start | bytes 2703360 | tf_op jit(solution)/shard_map/all_gather | solution.py:71
  435.2 435.6 %all-gather.9.cloned.1.call-start = ((), (), s32[]{:S(2)}) async-start(), calls=%async_computation.3 | async-start | bytes 2703360 | tf_op jit(solution)/shard_map/all_gather | solution.py:65
  491.3 384.9 %all-to-all-start.1 = ((bf16[32,18,320]{2,1,0:T(8,128)(2,1)}), bf16[32,18,320]{2,1,0:T(8,128)(2,1)S(1)}, u32[]{:S(2)}, u32[]{:S(2)}) async-start(bf16[32,18,320]{2,1,0:T(8,128)(2,1)} %reshape.78), calls=%async_computation.1 | async-start | bytes 1179648 | tf_op jit(solution)/shard_map/all_to_all | solution.py:54
  503.6 536.8 %all-reduce.4.cloned.1.call-start = ((), (), s32[]{:S(2)}) async-start(), calls=%async_computation.5 | async-start | bytes 983040 | tf_op jit(solution)/shard_map/psum | solution.py:75
  617.0 259.0 %copy-start.5 = (f32[48,6]{0,1:T(8,128)S(1)}, f32[48,6]{0,1:T(8,128)}, u32[]{:S(2)}) copy-start(f32[48,6]{0,1:T(8,128)} %param.13) | copy-start | bytes 3460
  876.0 164.4 %copy-start.3 = (bf16[48,320]{1,0:T(8,128)(2,1)S(1)}, bf16[48,320]{1,0:T(8,128)(2,1)}, u32[]{:S(2)}) copy-start(bf16[48,320]{1,0:T(8,128)(2,1)} %param.11) | copy-start | bytes 92164
  1041.2 27.8 %copy-start.4 = (bf16[48,320]{1,0:T(8,128)(2,1)}, bf16[48,320]{1,0:T(8,128)(2,1)S(1)}, u32[]{:S(2)}) copy-start(bf16[48,320]{1,0:T(8,128)(2,1)S(1)} %add_convert_fusion) | copy-start | bytes 92164
Sparse Core Ops, SparseCore 0:
  433.8 53.3 all-gather.12
  489.3 125.3 all-gather.6
  616.8 123.8 all-gather.10
  742.6 128.1 all-gather.8
  876.1 164.1 all-reduce.3
where the time goes:
time: 1080 us
  waiting for transfers between devices  580 us (54%)
  blocking collectives  416 us (39%)
  local copies, waits for them, and re-layouts  32.6 us (3%)
  matrix products  19.7 us (2%)
  between operations  14 us (1%)
  starting transfers between devices  12.7 us (1%)
    all_to_all x1, blocking collectives, per_device(): lax.all_to_all(outgoing, 'expert', split_axis=0, concat_axis=0, tiled=True)  359 us
    psum x1, waiting for transfers between devices, per_device(): lax.psum(shared_terms.astype(jnp.bfloat16), 'tensor').astype(jnp.float32)  162 us
    all_gather x1, waiting for transfers between devices, per_device(): lax.all_gather(shared_up, 'expert', axis=0, tiled=True)  130 us
    all_gather x1, waiting for transfers between devices, per_device(): lax.all_gather(shared_down, 'expert', axis=1, tiled=True)  124 us
    all_gather x1, waiting for transfers between devices, per_device(): lax.all_gather(shared_gate, 'expert', axis=0, tiled=True)  111 us
    all_gather x1, waiting for transfers between devices, per_device(): hidden_all = lax.all_gather(hidden, 'tensor', axis=1, tiled=True)  51.4 us
    all_gather x1, blocking collectives, per_device(): features = lax.all_gather(tokens, 'tensor', axis=1, tiled=True)  29.4 us
    all_gather x1, blocking collectives, per_device(): stream_all = lax.all_gather(stream, 'tensor', axis=1, tiled=True)  27.8 us
  transfers between devices with their start and end apart: 6, of which 5 were waited for; matrix products, arithmetic and copies ran while one was open for 1% of the time, Pallas kernels for 0%

commit v1 on v0

--- a/solution.py
+++ b/solution.py
@@ -72,7 +72,9 @@
         preferred_element_type=jnp.float32,
     )
     rank = lax.axis_index("tensor")
-    shared_full = lax.psum(shared_terms.astype(jnp.bfloat16), "tensor").astype(jnp.float32)
+    shared_full = jnp.sum(
+        lax.all_gather(shared_terms.astype(jnp.bfloat16), "tensor"), axis=0
+    ).astype(jnp.float32)
     shared_mine = lax.dynamic_slice_in_dim(shared_full, rank * local_width, local_width, 1)
     stream = (tokens.astype(jnp.float32) + shared_mine + routed).astype(jnp.bfloat16)
     stream_all = lax.all_gather(stream, "tensor", axis=1, tiled=True)

time: 1080 us -> 842 us (0.78)
  blocking collectives: 416 us -> 51.7 us
  waiting for transfers between devices: 580 us -> 689 us
  starting transfers between devices: 12.7 us -> 27.2 us
    all_to_all x0 -> x1, waiting for transfers between devices: none -> 375 us  [per_device(): lax.all_to_all(outgoing, 'expert', split_axis=0, concat_axis=0, tiled=True)]
    all_to_all x1 -> x0, blocking collectives: 359 us -> none  [per_device(): lax.all_to_all(outgoing, 'expert', split_axis=0, concat_axis=0, tiled=True)]
    psum x1 -> x0, waiting for transfers between devices: 162 us -> none  [per_device(): lax.psum(shared_terms.astype(jnp.bfloat16), 'tensor').astype(jnp.float32)]
    all_gather x1, waiting for transfers between devices: 111 us -> 0.02 us  [per_device(): lax.all_gather(shared_gate, 'expert', axis=0, tiled=True)]
    all_gather x1, waiting for transfers between devices: 130 us -> 42.3 us  [per_device(): lax.all_gather(shared_up, 'expert', axis=0, tiled=True)]
    all_gather x0 -> x1, waiting for transfers between devices: none -> 73.7 us  [per_device(): lax.all_gather(shared_terms.astype(jnp.bfloat16), 'tensor')]
    all_gather x1, waiting for transfers between devices: 51.4 us -> 74.7 us  [per_device(): hidden_all = lax.all_gather(hidden, 'tensor', axis=1, tiled=True)]
    all_to_all x0 -> x1, starting transfers between devices: none -> 14.6 us  [per_device(): lax.all_to_all(outgoing, 'expert', split_axis=0, concat_axis=0, tiled=True)]
  transfers between devices with their start and end apart: 6 -> 7, of which waited for: 5 -> 5; matrix products, arithmetic and copies ran while one was open for 1% -> 4% of each run, Pallas kernels for 0% -> 0%
where the time goes in v1:
time: 842 us
  waiting for transfers between devices  689 us (82%)
  blocking collectives  51.7 us (6%)
  local copies, waits for them, and re-layouts  32.4 us (4%)
  starting transfers between devices  27.2 us (3%)
  matrix products  19.7 us (2%)
  between operations  14.1 us (2%)
    all_to_all x1, waiting for transfers between devices, per_device(): lax.all_to_all(outgoing, 'expert', split_axis=0, concat_axis=0, tiled=True)  375 us
    all_gather x1, waiting for transfers between devices, per_device(): lax.all_gather(shared_down, 'expert', axis=1, tiled=True)  121 us
    all_gather x1, waiting for transfers between devices, per_device(): hidden_all = lax.all_gather(hidden, 'tensor', axis=1, tiled=True)  74.7 us
    all_gather x1, waiting for transfers between devices, per_device(): lax.all_gather(shared_terms.astype(jnp.bfloat16), 'tensor')  73.7 us
    all_gather x1, waiting for transfers between devices, per_device(): lax.all_gather(shared_up, 'expert', axis=0, tiled=True)  42.3 us
    all_gather x1, blocking collectives, per_device(): features = lax.all_gather(tokens, 'tensor', axis=1, tiled=True)  29.4 us
    all_gather x1, blocking collectives, per_device(): stream_all = lax.all_gather(stream, 'tensor', axis=1, tiled=True)  22.3 us
  transfers between devices with their start and end apart: 7, of which 5 were waited for; matrix products, arithmetic and copies ran while one was open for 4% of the time, Pallas kernels for 0%

profile of v1, /device:TPU:1, one launch (start us, length us, event | category | flops | bytes accessed | tf_op | source)
XLA Modules:
  0.0 841.5 jit_solution(11906436918319535641)
XLA Ops:
  7.2 0.9 copy.26
  8.1 0.7 broadcast_multiply_fusion
  8.9 0.9 reduce-window.6
  10.5 2.9 scatter_custom_fusion
  13.5 29.4 %all-gather.1 = bf16[16,320,48]{1,2,0:T(8,128)(2,1)S(1)} all-gather(bf16[1,320,48]{1,2,0:T(8,128)(2,1)} %bitcast.45), channel_id=1, replica_groups=mesh['expert'=32,'tensor'=16] {'tensor'}, dimensions={0}, use_global_device_ids=true | all-gather | bytes 522240 | tf_op jit(solution)/shard_map/all_gather | solution.py:35
  43.0 0.4 reshape.109
  43.5 6.0 gather_fusion
  49.5 8.4 reshape.76
  57.9 14.6 %all-to-all-start = ((bf16[32,18,5120]{2,1,0:T(8,128)(2,1)}), bf16[32,18,5120]{2,1,0:T(8,128)(2,1)}, u32[]{:S(2)}, u32[]{:S(2)}) async-start(bf16[32,18,5120]{2,1,0:T(8,128)(2,1)} %reshape.76), calls=%async_computation | async-start | bytes 15728640 | tf_op jit(solution)/shard_map/all_to_all | solution.py:47
  72.5 0.7 all-gather.9.cloned.1.call-update
  73.2 0.7 all-gather.11.cloned.1.call-update
  74.0 0.7 all-gather.13.cloned.1.call-update
  74.7 375.4 %all-to-all-done = bf16[32,18,5120]{2,1,0:T(8,128)(2,1)} async-done(((bf16[32,18,5120]{2,1,0:T(8,128)(2,1)}), bf16[32,18,5120]{2,1,0:T(8,128)(2,1)}, u32[]{:S(2)}, u32[]{:S(2)}) %all-to-all-start) | async-done | bytes 5898272 | tf_op jit(solution)/shard_map/all_to_all | solution.py:47
  450.1 8.8 %reshape.77 = bf16[576,5120]{1,0:T(8,128)(2,1)} reshape(bf16[32,18,5120]{2,1,0:T(8,128)(2,1)} %all-to-all-done) | data formatting | bytes 11796480 | tf_op jit(solution)/shard_map/reshape | solution.py:49
  458.9 4.8 fusion.4
  463.7 2.6 fusion
  466.5 2.3 fusion.20
  468.8 42.3 %all-gather.11.cloned.1.call-done = bf16[5120,192]{1,0:T(8,128)(2,1)} async-done(((bf16[160,192]{1,0:T(8,128)(2,1)}), bf16[5120,192]{1,0:T(8,128)(2,1)}) %all-gather.11.cloned.1.call-update) | async-done | bytes 1966096 | tf_op jit(solution)/shard_map/all_gather | solution.py:65
  511.1 121.2 %all-gather.13.cloned.1.call-done = bf16[192,5120]{0,1:T(8,128)(2,1)} async-done(((bf16[192,160]{0,1:T(8,128)(2,1)}), bf16[192,5120]{0,1:T(8,128)(2,1)}) %all-gather.13.cloned.1.call-update) | async-done | bytes 1966096 | tf_op jit(solution)/shard_map/all_gather | solution.py:71
  632.3 5.2 convolution_convert_fusion
  637.6 74.7 %all-gather.15.cloned.1.call-done = bf16[576,1536]{0,1:T(8,128)(2,1)} async-done(((bf16[576,96]{0,1:T(8,128)(2,1)}), bf16[576,1536]{0,1:T(8,128)(2,1)}) %all-gather.15.cloned.1.call-update) | async-done | bytes 1769488 | tf_op jit(solution)/shard_map/all_gather | solution.py:51
  712.2 2.8 convolution_convert_fusion.1
  715.0 0.2 copy.29
  715.3 1.0 reshape.78
  716.3 12.5 %all-to-all-start.1 = ((bf16[32,18,320]{2,1,0:T(8,128)(2,1)}), bf16[32,18,320]{2,1,0:T(8,128)(2,1)S(1)}, u32[]{:S(2)}, u32[]{:S(2)}) async-start(bf16[32,18,320]{2,1,0:T(8,128)(2,1)} %reshape.78), calls=%async_computation.1 | async-start | bytes 1179648 | tf_op jit(solution)/shard_map/all_to_all | solution.py:54
  728.9 73.7 %all-gather.17.cloned.1.call-done = bf16[768,5120]{1,0:T(8,128)(2,1)} async-done(((bf16[48,5120]{1,0:T(8,128)(2,1)}), bf16[768,5120]{1,0:T(8,128)(2,1)}) %all-gather.17.cloned.1.call-update) | async-done | bytes 7864336 | tf_op jit(solution)/shard_map/all_gather | solution.py:76
  802.6 4.8 reduce_sum.41
  807.6 2.0 gather_fusion.1
  809.7 0.2 multiply_reduce_fusion.1
  810.0 22.3 %all-gather.2 = bf16[16,320,48]{1,2,0:T(8,128)(2,1)S(1)} all-gather(bf16[1,320,48]{1,2,0:T(8,128)(2,1)S(1)} %bitcast.46), channel_id=1, replica_groups=mesh['expert'=32,'tensor'=16] {'tensor'}, dimensions={0}, use_global_device_ids=true | all-gather | bytes 522240 | tf_op jit(solution)/shard_map/all_gather | solution.py:80
  832.5 0.3 reshape.112
  833.0 2.0 convolution_convert_fusion.2
  (47 shorter events, 2.1 us)
Async XLA Ops:
  7.2 825.9 %copy-start = (bf16[132,5120]{1,0:T(8,128)(2,1)S(1)}, bf16[132,5120]{1,0:T(8,128)(2,1)}, u32[]{:S(2)}) copy-start(bf16[132,5120]{1,0:T(8,128)(2,1)} %param.21) | copy-start | bytes 4055044
  57.9 392.2 %all-to-all-start = ((bf16[32,18,5120]{2,1,0:T(8,128)(2,1)}), bf16[32,18,5120]{2,1,0:T(8,128)(2,1)}, u32[]{:S(2)}, u32[]{:S(2)}) async-start(bf16[32,18,5120]{2,1,0:T(8,128)(2,1)} %reshape.76), calls=%async_computation | async-start | bytes 15728640 | tf_op jit(solution)/shard_map/all_to_all | solution.py:47
  72.4 394.0 %all-gather.9.cloned.1.call-start = ((), (), s32[]{:S(2)}) async-start(), calls=%async_computation.2 | async-start | bytes 2703360 | tf_op jit(solution)/shard_map/all_gather | solution.py:60
  73.2 437.9 %all-gather.11.cloned.1.call-start = ((), (), s32[]{:S(2)}) async-start(), calls=%async_computation.3 | async-start | bytes 2703360 | tf_op jit(solution)/shard_map/all_gather | solution.py:65
  73.9 558.4 %all-gather.13.cloned.1.call-start = ((), (), s32[]{:S(2)}) async-start(), calls=%async_computation.4 | async-start | bytes 2703360 | tf_op jit(solution)/shard_map/all_gather | solution.py:71
  74.7 384.2 %copy-start.2 = (bf16[1,96,5120]{2,1,0:T(8,128)(2,1)S(1)}, bf16[1,96,5120]{2,1,0:T(8,128)(2,1)}, u32[]{:S(2)}) copy-start(bf16[1,96,5120]{2,1,0:T(8,128)(2,1)} %param.14) | copy-start | bytes 2949124
  74.7 637.5 %all-gather.15.cloned.1.call-start = ((), (), s32[]{:S(2)}) async-start(), calls=%async_computation.5 | async-start | bytes 2088960 | tf_op jit(solution)/shard_map/all_gather | solution.py:51
  458.9 4.8 copy-start.1
  458.9 4.8 copy-start.6
  466.4 336.2 %all-gather.17.cloned.1.call-start = ((), (), s32[]{:S(2)}) async-start(), calls=%async_computation.6 | async-start | bytes 8355840 | tf_op jit(solution)/shard_map/all_gather | solution.py:76
  715.0 13.8 %copy-start.5 = (f32[48,6]{0,1:T(8,128)S(1)}, f32[48,6]{0,1:T(8,128)}, u32[]{:S(2)}) copy-start(f32[48,6]{0,1:T(8,128)} %param.13) | copy-start | bytes 3460
  716.3 91.1 %all-to-all-start.1 = ((bf16[32,18,320]{2,1,0:T(8,128)(2,1)}), bf16[32,18,320]{2,1,0:T(8,128)(2,1)S(1)}, u32[]{:S(2)}, u32[]{:S(2)}) async-start(bf16[32,18,320]{2,1,0:T(8,128)(2,1)} %reshape.78), calls=%async_computation.1 | async-start | bytes 1179648 | tf_op jit(solution)/shard_map/all_to_all | solution.py:54
  807.3 2.6 copy-start.3
  810.0 22.3 %copy-start.4 = (bf16[48,320]{1,0:T(8,128)(2,1)}, bf16[48,320]{1,0:T(8,128)(2,1)S(1)}, u32[]{:S(2)}) copy-start(bf16[48,320]{1,0:T(8,128)(2,1)S(1)} %add_convert_fusion) | copy-start | bytes 92164
Sparse Core Ops, SparseCore 0:
  75.4 262.2 all-gather.8
  339.8 171.3 all-gather.10
  513.2 119.0 all-gather.12
  635.5 76.6 all-gather.14
  715.4 87.1 all-gather.16
